TPU v7x, 256 devices: a whole 4x4x8 slice. The times are simulated.
256 devices in a mesh: enc: 4 (over z_hi, core), dec: 4 (over z_lo), dp: 16 (over x, y).
Axes of the slice: x: 4, y: 4, z: 8 (z_hi: 2, z_lo: 4; z = z_hi * 4 + z_lo), core: 2. Of those that a mesh axis runs over, the one named last changes fastest.
Arguments:
- src_embed: bfloat16 [4, 128, 4096], P('dec'), may hold values from -8 to 8
- tgt_embed: bfloat16 [4, 128, 4096], P('enc'), may hold values from -8 to 8
- src_lengths: int32 [4], replicated, may hold values from 32 to 128
- enc_gain: float32 [4, 4096], P('enc'), may hold values from 0.1 to 1.9
- enc_project: bfloat16 [4, 4096, 3, 4096], P('enc', 'dec', None, 'dp'), may hold values from -0.09375 to 0.09375
- enc_output: bfloat16 [4, 4096, 4096], P('enc', 'dp', 'dec'), may hold values from -0.09375 to 0.09375
- final_gain: float32 [4096], replicated, may hold values from 0.1 to 1.9
- dec_gain: float32 [4, 4096], P('dec'), may hold values from 0.3 to 3
- dec_query: bfloat16 [4, 4096, 4096], P('dec', 'enc', 'dp'), may hold values from -0.09375 to 0.09375
- dec_memory: bfloat16 [4, 4096, 2, 4096], P('dec', 'enc', None, 'dp'), may hold values from -0.09375 to 0.09375
- dec_output: bfloat16 [4, 4096, 4096], P('dec', 'dp', 'enc'), may hold values from -0.09375 to 0.09375
Outputs:
- enc_states: bfloat16 [4, 4, 128, 4096], P('enc', 'dec')
- dec_states: bfloat16 [4, 4, 128, 4096], P('dec', 'enc')
All inputs are finite; a program needn't handle non-finite values.
Results may differ from a plain program's by a relative error of at most 0.035.
Values may be sent and summed in bfloat16 or wider, within the bound.
No kernel may reach another device: no remote copies, remote signals or barrier semaphores. Data moves between devices by JAX's collectives and lax.ppermute only.
A program may use at most 64 MiB of HBM per device.

v0:
```python
import math

import jax
import jax.numpy as jnp
from jax import lax
from jax.sharding import PartitionSpec as P

HD = 256


def passed_along(x, axis, by):
    count = lax.axis_size(axis)
    pairs = [(i, i + by) for i in range(count) if 0 <= i + by < count]
    return lax.ppermute(x, axis, pairs)


def spread(x, axis, root):
    mine = lax.axis_index(axis) == root
    return lax.psum(jnp.where(mine, x, jnp.zeros_like(x)), axis)


def normalize(values, gain):
    wide = values.astype(jnp.float32)
    return wide * lax.rsqrt(jnp.mean(wide * wide, axis=-1, keepdims=True) + 1e-06) * gain


def attend(query, keys, values, length):
    rows = query.shape[0]
    span = keys.shape[0]
    query_heads = query.reshape(rows, -1, HD)
    key_heads = keys.reshape(span, -1, HD)
    value_heads = values.reshape(span, -1, HD)
    scores = jnp.einsum(
        "rhc,shc->hrs", query_heads, key_heads, preferred_element_type=jnp.float32
    ) * (1.0 / math.sqrt(HD))
    valid = jnp.arange(span) < length
    scores = jnp.where(valid[None, None, :], scores, -1e30)
    top = jnp.max(scores, axis=-1, keepdims=True)
    weights = jnp.exp(scores - top)
    probs = (weights / jnp.sum(weights, axis=-1, keepdims=True)).astype(jnp.bfloat16)
    mixed = jnp.einsum("hrs,shc->rhc", probs, value_heads, preferred_element_type=jnp.float32)
    return mixed.astype(jnp.bfloat16).reshape(rows, -1)


def pick_length(table, position):
    return jnp.sum(jnp.where(jnp.arange(table.shape[0]) == position, table, 0))


def split_mixed(mixed, memory_pair):
    if memory_pair is None:
        return (mixed[:, 0], mixed[:, 1], mixed[:, 2])
    return (mixed[:, 0], memory_pair[0], memory_pair[1])


def project_rows(piece, weight):
    return jnp.einsum("rd,dkc->rkc", piece, weight, preferred_element_type=jnp.float32).astype(
        jnp.bfloat16
    )


def on_device(
    src_embed,
    tgt_embed,
    src_lengths,
    enc_gain,
    enc_project,
    enc_output,
    final_gain,
    dec_gain,
    dec_query,
    dec_memory,
    dec_output,
):
    sections_enc = lax.axis_size("enc")
    sections_dec = lax.axis_size("dec")
    enc_place = lax.axis_index("enc")
    dec_place = lax.axis_index("dec")
    src_rows = src_embed[0]
    tgt_rows = tgt_embed[0]
    enc_length = pick_length(src_lengths, dec_place)
    dec_length = pick_length(src_lengths, enc_place)
    enc_weight_in, enc_weight_out = (
        lax.all_gather(enc_project[0], "dec", axis=0, tiled=True),
        lax.all_gather(enc_output[0], "dec", axis=1, tiled=True),
    )
    dec_weight_query, dec_weight_memory, dec_weight_out = (
        lax.all_gather(dec_query[0], "enc", axis=0, tiled=True),
        lax.all_gather(dec_memory[0], "enc", axis=0, tiled=True),
        lax.all_gather(dec_output[0], "enc", axis=1, tiled=True),
    )
    enc_start, dec_start = (src_rows, tgt_rows)

    def sublayer(current, gain, weight_in, weight_out, length, memory_pair):
        normed = normalize(current, gain).astype(jnp.bfloat16)
        mixed = project_rows(normed, weight_in)
        query, keys, values = split_mixed(mixed, memory_pair)
        attended = attend(query, keys, values, length)
        partial_sum = jnp.dot(attended, weight_out, preferred_element_type=jnp.float32)
        summed = lax.psum(partial_sum.astype(jnp.bfloat16), "dp").astype(jnp.float32)
        return (current.astype(jnp.float32) + summed).astype(jnp.bfloat16)

    current = enc_start
    enc_state = enc_start
    for step in range(sections_enc):
        result = sublayer(current, enc_gain[0], enc_weight_in, enc_weight_out, enc_length, None)
        enc_state = jnp.where(enc_place == step, result, enc_state)
        if step + 1 < sections_enc:
            current = passed_along(result, "enc", 1)
    memory = normalize(enc_state, final_gain).astype(jnp.bfloat16)
    memory = spread(memory, "enc", sections_enc - 1)
    memory = spread(memory, "dec", enc_place)
    pairs = project_rows(memory, dec_weight_memory)
    memory_pair = (pairs[:, 0], pairs[:, 1])
    current = dec_start
    dec_state = dec_start
    query_weight = dec_weight_query[:, None, :]
    for step in range(sections_dec):
        result = sublayer(
            current, dec_gain[0], query_weight, dec_weight_out, dec_length, memory_pair
        )
        dec_state = jnp.where(dec_place == step, result, dec_state)
        if step + 1 < sections_dec:
            current = passed_along(result, "dec", 1)
    return (enc_state[None, None], dec_state[None, None])


def solution(mesh):
    placed = (
        P("dec", None, None),
        P("enc", None, None),
        P(),
        P("enc", None),
        P("enc", "dec", None, "dp"),
        P("enc", "dp", "dec"),
        P(),
        P("dec", None),
        P("dec", "enc", "dp"),
        P("dec", "enc", None, "dp"),
        P("dec", "dp", "enc"),
    )
    return jax.shard_map(
        on_device,
        mesh=mesh,
        in_specs=placed,
        out_specs=(P("enc", "dec", None, None), P("dec", "enc", None, None)),
        check_vma=False,
    )
```

profile of v0, /device:TPU:32, one launch (start us, length us, event | category | flops | bytes accessed | tf_op | source)
XLA Modules:
  0.0 1475.2 jit_solution(6102132343366791482)
XLA Ops:
  8.0 0.7 all-gather.13.cloned.1.call-update
  8.7 0.7 fusion.202
  10.4 120.6 %all-gather.11.cloned.1.call-done = bf16[1,4096,3,256]{3,1,2,0:T(8,128)(2,1)} async-done(((bf16[1,1024,3,256]{3,1,2,0:T(8,128)(2,1)}), bf16[1,4096,3,256]{3,1,2,0:T(8,128)(2,1)}) %all-gather.11.cloned.1.call-update) | async-done | bytes 6291472 | tf_op jit(solution)/shard_map/all_gather | solution.py:83
  131.0 3.8 fusion.59
  135.1 47.0 %all-gather.13.cloned.1.call-done = bf16[1,256,4096]{2,1,0:T(8,128)(2,1)} async-done(((bf16[1,256,1024]{2,1,0:T(8,128)(2,1)}), bf16[1,256,4096]{2,1,0:T(8,128)(2,1)}) %all-gather.13.cloned.1.call-update) | async-done | bytes 2097168 | tf_op jit(solution)/shard_map/all_gather | solution.py:84
  182.1 3.2 convolution_convert_fusion.7
  185.4 98.2 %all-reduce.11.cloned.1.call-done = bf16[128,4096]{1,0:T(8,128)(2,1)} async-done(((bf16[128,4096]{1,0:T(8,128)(2,1)}), bf16[128,4096]{1,0:T(8,128)(2,1)}) %all-reduce.11.cloned.1.call-update) | async-done | bytes 1048592 | tf_op jit(solution)/shard_map/psum | solution.py:99
  283.6 1.5 fusion.18
  285.0 1.4 collective-permute-start
  286.4 2.2 collective-permute-done
  288.9 4.0 fusion.62
  293.2 1.6 convolution_convert_fusion.6
  294.9 123.4 %all-reduce.13.cloned.1.call-done = bf16[128,4096]{1,0:T(8,128)(2,1)} async-done(((bf16[128,4096]{1,0:T(8,128)(2,1)}), bf16[128,4096]{1,0:T(8,128)(2,1)}) %all-reduce.13.cloned.1.call-update) | async-done | bytes 1048592 | tf_op jit(solution)/shard_map/psum | solution.py:99
  418.3 1.8 fusion.22
  420.1 1.4 collective-permute-start.1
  421.5 2.2 collective-permute-done.1
  424.0 3.9 fusion.65
  428.2 1.6 convolution_convert_fusion.5
  429.9 123.4 %all-reduce.15.cloned.1.call-done = bf16[128,4096]{1,0:T(8,128)(2,1)} async-done(((bf16[128,4096]{1,0:T(8,128)(2,1)}), bf16[128,4096]{1,0:T(8,128)(2,1)}) %all-reduce.15.cloned.1.call-update) | async-done | bytes 1048592 | tf_op jit(solution)/shard_map/psum | solution.py:99
  553.4 1.8 fusion.26
  555.2 1.0 copy-done.10
  556.1 1.3 collective-permute-start.2
  557.5 2.2 collective-permute-done.2
  560.0 3.9 fusion.68
  564.2 1.6 convolution_convert_fusion.4
  565.9 123.4 %all-reduce.17.cloned.1.call-done = bf16[128,4096]{1,0:T(8,128)(2,1)} async-done(((bf16[128,4096]{1,0:T(8,128)(2,1)}), bf16[128,4096]{1,0:T(8,128)(2,1)}) %all-reduce.17.cloned.1.call-update) | async-done | bytes 1048592 | tf_op jit(solution)/shard_map/psum | solution.py:99
  689.3 2.9 fusion.12
  692.2 0.9 copy-done.14
  693.2 1.4 fusion.130
  694.7 1.1 copy.13
  695.9 67.7 %all-reduce.19.cloned.1.call-done = bf16[128,4096]{1,0:T(8,128)(2,1)} async-done(((bf16[128,4096]{1,0:T(8,128)(2,1)}), bf16[128,4096]{1,0:T(8,128)(2,1)}) %all-reduce.19.cloned.1.call-update) | async-done | bytes 1048592 | tf_op jit(solution)/shard_map/psum | solution.py:19
  763.5 1.0 broadcast_select_fusion
  765.2 0.7 all-gather.19.cloned.1.call-update
  767.2 65.1 %all-gather.15.cloned.1.call-done = bf16[1,4096,2,256]{3,1,2,0:T(8,128)(2,1)} async-done(((bf16[1,1024,2,256]{3,1,2,0:T(8,128)(2,1)}), bf16[1,4096,2,256]{3,1,2,0:T(8,128)(2,1)}) %all-gather.15.cloned.1.call-update) | async-done | bytes 4194320 | tf_op jit(solution)/shard_map/all_gather | solution.py:88
  832.2 62.3 %all-reduce.21.cloned.1.call-done = bf16[128,4096]{1,0:T(8,128)(2,1)} async-done(((bf16[128,4096]{1,0:T(8,128)(2,1)}), bf16[128,4096]{1,0:T(8,128)(2,1)}) %all-reduce.21.cloned.1.call-update) | async-done | bytes 1048592 | tf_op jit(solution)/shard_map/psum | solution.py:19
  894.5 3.2 fusion.71
  897.7 41.3 %all-gather.17.cloned.1.call-done = bf16[1,4096,256]{2,1,0:T(8,128)(2,1)} async-done(((bf16[1,1024,256]{2,1,0:T(8,128)(2,1)}), bf16[1,4096,256]{2,1,0:T(8,128)(2,1)}) %all-gather.17.cloned.1.call-update) | async-done | bytes 2097168 | tf_op jit(solution)/shard_map/all_gather | solution.py:87
  939.1 2.3 fusion.208
  941.4 39.0 %all-gather.19.cloned.1.call-done = bf16[1,256,4096]{2,1,0:T(8,128)(2,1)} async-done(((bf16[1,256,1024]{2,1,0:T(8,128)(2,1)}), bf16[1,256,4096]{2,1,0:T(8,128)(2,1)}) %all-gather.19.cloned.1.call-update) | async-done | bytes 2097168 | tf_op jit(solution)/shard_map/all_gather | solution.py:89
  980.4 3.2 convolution_convert_fusion.3
  983.7 95.1 %all-reduce.23.cloned.1.call-done = bf16[128,4096]{1,0:T(8,128)(2,1)} async-done(((bf16[128,4096]{1,0:T(8,128)(2,1)}), bf16[128,4096]{1,0:T(8,128)(2,1)}) %all-reduce.23.cloned.1.call-update) | async-done | bytes 1048592 | tf_op jit(solution)/shard_map/psum | solution.py:99
  1078.8 1.5 fusion.11
  1080.3 3.5 collective-permute-start.3
  1083.8 21.8 %collective-permute-done.3 = bf16[128,4096]{1,0:T(8,128)(2,1)S(1)} collective-permute-done((bf16[128,4096]{1,0:T(8,128)(2,1)S(1)}, bf16[128,4096]{1,0:T(8,128)(2,1)S(1)}, u32[]{:S(2)}, u32[]{:S(2)}) %collective-permute-start.3) | collective-permute-done | bytes 1048608 | tf_op jit(solution)/shard_map/ppermute | solution.py:14
  1105.6 1.0 copy-done.6
  1106.9 2.7 fusion.213
  1109.7 1.7 convolution_convert_fusion.2
  1111.4 95.6 %all-reduce.25.cloned.1.call-done = bf16[128,4096]{1,0:T(8,128)(2,1)} async-done(((bf16[128,4096]{1,0:T(8,128)(2,1)}), bf16[128,4096]{1,0:T(8,128)(2,1)}) %all-reduce.25.cloned.1.call-update) | async-done | bytes 1048592 | tf_op jit(solution)/shard_map/psum | solution.py:99
  1206.9 1.8 fusion.34
  1208.8 3.5 collective-permute-start.4
  1212.2 21.8 %collective-permute-done.4 = bf16[128,4096]{1,0:T(8,128)(2,1)S(1)} collective-permute-done((bf16[128,4096]{1,0:T(8,128)(2,1)S(1)}, bf16[128,4096]{1,0:T(8,128)(2,1)S(1)}, u32[]{:S(2)}, u32[]{:S(2)}) %collective-permute-start.4) | collective-permute-done | bytes 1048608 | tf_op jit(solution)/shard_map/ppermute | solution.py:14
  1234.0 1.0 copy-done.7
  1235.3 2.6 fusion.218
  1238.0 1.7 convolution_convert_fusion.1
  1239.7 95.6 %all-reduce.27.cloned.1.call-done = bf16[128,4096]{1,0:T(8,128)(2,1)} async-done(((bf16[128,4096]{1,0:T(8,128)(2,1)}), bf16[128,4096]{1,0:T(8,128)(2,1)}) %all-reduce.27.cloned.1.call-update) | async-done | bytes 1048592 | tf_op jit(solution)/shard_map/psum | solution.py:99
  1335.3 1.8 fusion.38
  1337.1 1.0 copy-done.11
  1338.1 3.5 collective-permute-start.5
  1341.5 21.8 %collective-permute-done.5 = bf16[128,4096]{1,0:T(8,128)(2,1)S(1)} collective-permute-done((bf16[128,4096]{1,0:T(8,128)(2,1)S(1)}, bf16[128,4096]{1,0:T(8,128)(2,1)S(1)}, u32[]{:S(2)}, u32[]{:S(2)}) %collective-permute-start.5) | collective-permute-done | bytes 1048608 | tf_op jit(solution)/shard_map/ppermute | solution.py:14
  1363.3 1.0 copy-done.13
  1364.6 2.6 fusion.223
  1367.3 1.6 convolution_convert_fusion
  1368.9 95.6 %all-reduce.29.cloned.1.call-done = bf16[128,4096]{1,0:T(8,128)(2,1)} async-done(((bf16[128,4096]{1,0:T(8,128)(2,1)}), bf16[128,4096]{1,0:T(8,128)(2,1)}) %all-reduce.29.cloned.1.call-update) | async-done | bytes 1048592 | tf_op jit(solution)/shard_map/psum | solution.py:99
  1464.6 4.1 fusion.114
  (93 shorter events, 7.0 us)
Async XLA Ops:
  7.2 1.6 copy-start.17
  7.2 2.9 copy-start.2
  7.2 123.9 %copy-start.18 = (f32[1,4096]{1,0:T(1,128)S(1)}, f32[1,4096]{1,0:T(1,128)}, u32[]{:S(2)}) copy-start(f32[1,4096]{1,0:T(1,128)} %param.14) | copy-start | bytes 49156
  7.2 123.8 %all-gather.11.cloned.1.call-start = ((), (), s32[]{:S(2)}) async-start(), calls=%async_computation.10 | async-start | bytes 7864320 | tf_op jit(solution)/shard_map/all_gather | solution.py:83
  7.9 174.1 %all-gather.13.cloned.1.call-start = ((), (), s32[]{:S(2)}) async-start(), calls=%async_computation.11 | async-start | bytes 2621440 | tf_op jit(solution)/shard_map/all_gather | solution.py:84
  8.7 274.9 %all-reduce.11.cloned.1.call-start = ((), (), s32[]{:S(2)}) async-start(), calls=%async_computation | async-start | bytes 2097152 | tf_op jit(solution)/shard_map/psum | solution.py:99
  185.3 233.0 %all-reduce.13.cloned.1.call-start = ((), (), s32[]{:S(2)}) async-start(), calls=%async_computation.1 | async-start | bytes 2097152 | tf_op jit(solution)/shard_map/psum | solution.py:99
  285.0 3.6 collective-permute-start
  288.6 4.3 copy-start.4
  288.9 4.3 copy-start
  294.9 258.5 %all-reduce.15.cloned.1.call-start = ((), (), s32[]{:S(2)}) async-start(), calls=%async_computation.2 | async-start | bytes 2097152 | tf_op jit(solution)/shard_map/psum | solution.py:99
  420.1 3.6 copy-start.8
  420.1 3.6 collective-permute-start.1
  423.7 4.2 copy-start.5
  429.9 259.4 %all-reduce.17.cloned.1.call-start = ((), (), s32[]{:S(2)}) async-start(), calls=%async_computation.3 | async-start | bytes 2097152 | tf_op jit(solution)/shard_map/psum | solution.py:99
  555.1 1.0 copy-start.10
  556.1 3.6 collective-permute-start.2
  559.7 4.2 copy-start.12
  565.8 197.7 %all-reduce.19.cloned.1.call-start = ((), (), s32[]{:S(2)}) async-start(), calls=%async_computation.4 | async-start | bytes 2097152 | tf_op jit(solution)/shard_map/psum | solution.py:19
  565.9 127.3 %copy-start.16 = (f32[4096]{0:T(1024)S(1)}, f32[4096]{0:T(1024)}, u32[]{:S(2)}) copy-start(f32[4096]{0:T(1024)} %param.17) | copy-start | bytes 49156
  692.2 1.0 copy-start.14
  692.2 2.4 copy-start.15
  694.6 137.6 %all-gather.15.cloned.1.call-start = ((), (), s32[]{:S(2)}) async-start(), calls=%async_computation.12 | async-start | bytes 5242880 | tf_op jit(solution)/shard_map/all_gather | solution.py:88
  695.8 198.7 %all-reduce.21.cloned.1.call-start = ((), (), s32[]{:S(2)}) async-start(), calls=%async_computation.5 | async-start | bytes 2097152 | tf_op jit(solution)/shard_map/psum | solution.py:19
  695.8 71.0 %copy-start.3 = (bf16[1,128,4096]{2,1,0:T(8,128)(2,1)S(1)}, bf16[1,128,4096]{2,1,0:T(8,128)(2,1)}, u32[]{:S(2)}) copy-start(bf16[1,128,4096]{2,1,0:T(8,128)(2,1)} %param.12) | copy-start | bytes 3145732
  764.6 174.5 %all-gather.17.cloned.1.call-start = ((), (), s32[]{:S(2)}) async-start(), calls=%async_computation.13 | async-start | bytes 2621440 | tf_op jit(solution)/shard_map/all_gather | solution.py:87
  765.2 215.3 %all-gather.19.cloned.1.call-start = ((), (), s32[]{:S(2)}) async-start(), calls=%async_computation.14 | async-start | bytes 2621440 | tf_op jit(solution)/shard_map/all_gather | solution.py:89
  765.9 312.9 %all-reduce.23.cloned.1.call-start = ((), (), s32[]{:S(2)}) async-start(), calls=%async_computation.6 | async-start | bytes 2097152 | tf_op jit(solution)/shard_map/psum | solution.py:99
  767.1 171.9 %copy-start.19 = (f32[1,4096]{1,0:T(1,128)S(1)}, f32[1,4096]{1,0:T(1,128)}, u32[]{:S(2)}) copy-start(f32[1,4096]{1,0:T(1,128)} %param.18) | copy-start | bytes 49156
  983.7 223.3 %all-reduce.25.cloned.1.call-start = ((), (), s32[]{:S(2)}) async-start(), calls=%async_computation.7 | async-start | bytes 2097152 | tf_op jit(solution)/shard_map/psum | solution.py:99
  1080.3 25.3 %collective-permute-start.3 = (bf16[128,4096]{1,0:T(8,128)(2,1)S(1)}, bf16[128,4096]{1,0:T(8,128)(2,1)S(1)}, u32[]{:S(2)}, u32[]{:S(2)}) collective-permute-start(bf16[128,4096]{1,0:T(8,128)(2,1)S(1)} %fusion.11), channel_id=1, source_target_pairs={{0,16},{16,32},{32,48},{1,17},{17,33},{33,49},{2,18},{18,34},{34,5... | collective-permute-start | bytes 3145736 | tf_op jit(solution)/shard_map/ppermute | solution.py:14
  1105.6 1.0 copy-start.6
  1106.8 2.8 copy-start.1
  1111.3 223.9 %all-reduce.27.cloned.1.call-start = ((), (), s32[]{:S(2)}) async-start(), calls=%async_computation.8 | async-start | bytes 2097152 | tf_op jit(solution)/shard_map/psum | solution.py:99
  1208.7 26.5 %copy-start.9 = (bf16[128,4096]{1,0:T(8,128)(2,1)}, bf16[128,4096]{1,0:T(8,128)(2,1)S(1)}, u32[]{:S(2)}) copy-start(bf16[128,4096]{1,0:T(8,128)(2,1)S(1)} %fusion.34) | copy-start | bytes 3145732
  1208.8 25.3 %collective-permute-start.4 = (bf16[128,4096]{1,0:T(8,128)(2,1)S(1)}, bf16[128,4096]{1,0:T(8,128)(2,1)S(1)}, u32[]{:S(2)}, u32[]{:S(2)}) collective-permute-start(bf16[128,4096]{1,0:T(8,128)(2,1)S(1)} %fusion.34), channel_id=1, source_target_pairs={{0,16},{16,32},{32,48},{1,17},{17,33},{33,49},{2,18},{18,34},{34,5... | collective-permute-start | bytes 3145736 | tf_op jit(solution)/shard_map/ppermute | solution.py:14
  1234.0 1.0 copy-start.7
  1239.6 224.9 %all-reduce.29.cloned.1.call-start = ((), (), s32[]{:S(2)}) async-start(), calls=%async_computation.9 | async-start | bytes 2097152 | tf_op jit(solution)/shard_map/psum | solution.py:99
  1337.1 1.0 copy-start.11
  1338.1 25.3 %collective-permute-start.5 = (bf16[128,4096]{1,0:T(8,128)(2,1)S(1)}, bf16[128,4096]{1,0:T(8,128)(2,1)S(1)}, u32[]{:S(2)}, u32[]{:S(2)}) collective-permute-start(bf16[128,4096]{1,0:T(8,128)(2,1)S(1)} %fusion.38), channel_id=1, source_target_pairs={{0,16},{16,32},{32,48},{1,17},{17,33},{33,49},{2,18},{18,34},{34,5... | collective-permute-start | bytes 3145736 | tf_op jit(solution)/shard_map/ppermute | solution.py:14
  1363.3 1.0 copy-start.13
Sparse Core Ops, SparseCore 0:
  9.8 121.1 all-gather.10
  132.8 49.1 all-gather.12
  185.9 97.6 all-reduce.10
  295.0 123.3 all-reduce.12
  430.0 123.3 all-reduce.14
  565.9 123.2 all-reduce.16
  694.7 68.7 all-reduce.18
  766.1 66.1 all-gather.14
  835.1 59.3 all-reduce.20
  896.2 42.8 all-gather.16
  940.9 39.5 all-gather.18
  984.1 94.6 all-reduce.22
  1111.5 95.4 all-reduce.24
  1239.8 95.4 all-reduce.26
  1369.1 95.4 all-reduce.28
where the time goes:
time: 1480 us
  waiting for transfers between devices  1370 us (93%)
  matrix products  46.3 us (3%)
  other arithmetic  24.3 us (2%)
  starting transfers between devices  15.2 us (1%)
    psum x8, waiting for transfers between devices, sublayer(): lax.psum(partial_sum.astype(jnp.bfloat16), 'dp').astype(jnp.float32)  850 us
    psum x2, waiting for transfers between devices, spread(): return lax.psum(jnp.where(mine, x, jnp.zeros_like(x)), axis)  130 us
    all_gather x1, waiting for transfers between devices, on_device(): lax.all_gather(enc_project[0], 'dec', axis=0, tiled=True)  121 us
    ppermute x6, waiting for transfers between devices, passed_along(): return lax.ppermute(x, axis, pairs)  72 us
    all_gather x1, waiting for transfers between devices, on_device(): lax.all_gather(dec_memory[0], 'enc', axis=0, tiled=True)  65.1 us
    all_gather x1, waiting for transfers between devices, on_device(): lax.all_gather(enc_output[0], 'dec', axis=1, tiled=True)  47 us
    all_gather x1, waiting for transfers between devices, on_device(): lax.all_gather(dec_query[0], 'enc', axis=0, tiled=True)  41.3 us
    all_gather x1, waiting for transfers between devices, on_device(): lax.all_gather(dec_output[0], 'enc', axis=1, tiled=True)  39 us
  transfers between devices with their start and end apart: 21, of which 21 were waited for; matrix products, arithmetic and copies ran while one was open for 1% of the time, Pallas kernels for 0%

commit v1 on v0

v1 whole, which is shorter than its diff:
```python
import math

import jax
import jax.numpy as jnp
from jax import lax
from jax.sharding import PartitionSpec as P

HD = 256
AXES = ("enc", "dec", "dp")


def normalize(values, gain):
    wide = values.astype(jnp.float32)
    return wide * lax.rsqrt(jnp.mean(wide * wide, axis=-1, keepdims=True) + 1e-06) * gain


def attend(query, keys, values, length):
    span = keys.shape[0]
    scores = lax.dot_general(
        query, keys, (((1,), (1,)), ((), ())), preferred_element_type=jnp.float32
    ) * (1.0 / math.sqrt(HD))
    valid = jnp.arange(span) < length
    scores = jnp.where(valid[None, :], scores, -1e30)
    top = jnp.max(scores, axis=-1, keepdims=True)
    weights = jnp.exp(scores - top)
    probs = (weights / jnp.sum(weights, axis=-1, keepdims=True)).astype(jnp.bfloat16)
    return jnp.dot(probs, values, preferred_element_type=jnp.float32).astype(jnp.bfloat16)


def pick_length(table, position):
    return jnp.sum(jnp.where(jnp.arange(table.shape[0]) == position, table, 0))


def project_rows(piece, weight):
    return jnp.einsum("rd,dkc->rkc", piece, weight, preferred_element_type=jnp.float32).astype(
        jnp.bfloat16
    )


def gather_rows(piece):
    count = lax.axis_size("dp")
    copies = jnp.broadcast_to(piece[None], (count,) + piece.shape)
    return lax.all_to_all(copies, "dp", 0, 0).reshape(-1, piece.shape[-1])


def scatter_sum(partial_sum):
    count = lax.axis_size("dp")
    blocks = partial_sum.reshape(count, -1, partial_sum.shape[-1])
    return jnp.sum(lax.all_to_all(blocks, "dp", 0, 0).astype(jnp.float32), axis=0)


def own_rows(full):
    rows = full.shape[0] // lax.axis_size("dp")
    return lax.dynamic_slice_in_dim(full, lax.axis_index("dp") * rows, rows, 0)


def on_device(
    src_embed,
    tgt_embed,
    src_lengths,
    enc_gain,
    enc_project,
    enc_output,
    final_gain,
    dec_gain,
    dec_query,
    dec_memory,
    dec_output,
):
    sections_enc = lax.axis_size("enc")
    sections_dec = lax.axis_size("dec")
    enc_place = lax.axis_index("enc")
    dec_place = lax.axis_index("dec")
    enc_length = pick_length(src_lengths, dec_place)
    dec_length = pick_length(src_lengths, enc_place)
    enc_weight_in = lax.all_gather(enc_project[0], "dec", axis=0, tiled=True)
    enc_weight_out = lax.all_gather(enc_output[0], "dec", axis=1, tiled=True)
    dec_weight_memory = lax.all_gather(dec_memory[0], "enc", axis=0, tiled=True)
    dec_weight_query = lax.all_gather(dec_query[0], "enc", axis=0, tiled=True)
    dec_weight_out = lax.all_gather(dec_output[0], "enc", axis=1, tiled=True)

    current = src_embed[0]
    piece = own_rows(current)
    enc_piece = piece
    for step in range(sections_enc):
        normed = normalize(current, enc_gain[0]).astype(jnp.bfloat16)
        mixed = project_rows(normed, enc_weight_in)
        attended = attend(mixed[:, 0], mixed[:, 1], mixed[:, 2], enc_length)
        partial_sum = jnp.dot(attended, enc_weight_out, preferred_element_type=jnp.float32)
        summed = scatter_sum(partial_sum.astype(jnp.bfloat16))
        result = (piece.astype(jnp.float32) + summed).astype(jnp.bfloat16)
        enc_piece = jnp.where(enc_place == step, result, enc_piece)
        if step + 1 < sections_enc:
            piece = lax.ppermute(result, "enc", [(step, step + 1)])
            current = gather_rows(piece)

    memory_piece = normalize(enc_piece, final_gain).astype(jnp.bfloat16)
    parts = lax.axis_size("dp")
    last = sections_enc - 1

    def place(e, d, p):
        return (e * sections_dec + d) * parts + p

    memory_here = jnp.zeros_like(memory_piece)
    for by in range(sections_dec):
        pairs = [
            (place(last, m, p), place(m, (m + by) % sections_dec, p))
            for m in range(sections_dec)
            for p in range(parts)
        ]
        pairs_moved = [(a, b) for a, b in pairs if a != b]
        memory_here = memory_here + lax.ppermute(memory_piece, AXES, pairs_moved)
    stays = (enc_place == last) & (dec_place == last)
    memory_here = jnp.where(stays, memory_piece, memory_here)
    memory = gather_rows(memory_here)
    pairs = project_rows(memory, dec_weight_memory)
    keys, values = pairs[:, 0], pairs[:, 1]

    current = tgt_embed[0]
    piece = own_rows(current)
    dec_piece = piece
    enc_state = lax.all_gather(enc_piece, "dp", axis=0, tiled=True)
    for step in range(sections_dec):
        if step == sections_dec - 1:
            current, enc_state = lax.optimization_barrier((current, enc_state))
        normed = normalize(current, dec_gain[0]).astype(jnp.bfloat16)
        query = jnp.dot(normed, dec_weight_query, preferred_element_type=jnp.float32)
        attended = attend(query.astype(jnp.bfloat16), keys, values, dec_length)
        partial_sum = jnp.dot(attended, dec_weight_out, preferred_element_type=jnp.float32)
        summed = scatter_sum(partial_sum.astype(jnp.bfloat16))
        result = (piece.astype(jnp.float32) + summed).astype(jnp.bfloat16)
        dec_piece = jnp.where(dec_place == step, result, dec_piece)
        if step + 1 < sections_dec:
            piece = lax.ppermute(result, "dec", [(step, step + 1)])
            current = gather_rows(piece)
    dec_state = gather_rows(dec_piece)
    return (enc_state[None, None], dec_state[None, None])


def solution(mesh):
    placed = (
        P("dec", None, None),
        P("enc", None, None),
        P(),
        P("enc", None),
        P("enc", "dec", None, "dp"),
        P("enc", "dp", "dec"),
        P(),
        P("dec", None),
        P("dec", "enc", "dp"),
        P("dec", "enc", None, "dp"),
        P("dec", "dp", "enc"),
    )
    return jax.shard_map(
        on_device,
        mesh=mesh,
        in_specs=placed,
        out_specs=(P("enc", "dec", None, None), P("dec", "enc", None, None)),
        check_vma=False,
    )
```

time: 1480 us -> 618 us (0.42)
  waiting for transfers between devices: 1370 us -> 352 us
  blocking collectives: 0 us -> 135 us
  starting transfers between devices: 15.2 us -> 49.5 us
  other arithmetic: 24.3 us -> 8.14 us
    psum x10 -> x0, waiting for transfers between devices: 980 us -> none  [the longest x8 850 us: sublayer(): lax.psum(partial_sum.astype(jnp.bfloat16), 'dp').astype(jnp.float32)]
    all_to_all x0 -> x7, blocking collectives: none -> 135 us  [the longest x4 72 us: gather_rows(): return lax.all_to_all(copies, 'dp', 0, 0).reshape(-1, piece.shape[-1])]
    all_to_all x0 -> x9, waiting for transfers between devices: none -> 120 us  [the longest x5 76.9 us: scatter_sum(): lax.all_to_all(blocks, 'dp', 0, 0).astype(jnp.float32)]
    all_gather x5 -> x6, waiting for transfers between devices: 313 us -> 208 us  [the longest x1 121 us: on_device(): enc_weight_in = lax.all_gather(enc_project[0], 'dec', axis=0, tiled=True)]
    ppermute x6 -> x10, waiting for transfers between devices: 72 us -> 21.2 us  [the longest x4 13.5 us: on_device(): memory_here = memory_here + lax.ppermute(memory_piece, AXES, pairs_moved)]
    all_to_all x0 -> x9, starting transfers between devices: none -> 40.1 us  [the longest x5 25.3 us: scatter_sum(): lax.all_to_all(blocks, 'dp', 0, 0).astype(jnp.float32)]
  transfers between devices with their start and end apart: 21 -> 25, of which waited for: 21 -> 16; matrix products, arithmetic and copies ran while one was open for 1% -> 5% of each run, Pallas kernels for 0% -> 0%
where the time goes in v1:
time: 618 us; the launch traced here: 616 us
  waiting for transfers between devices  352 us (57%)
  blocking collectives  135 us (22%)
  starting transfers between devices  49.5 us (8%)
  matrix products  43.8 us (7%)
  between operations  16.1 us (3%)
  local copies, waits for them, and re-layouts  11.3 us (2%)
  other arithmetic  8.14 us (1%)
    all_gather x1, waiting for transfers between devices, on_device(): enc_weight_in = lax.all_gather(enc_project[0], 'dec', axis=0, tiled=True)  121 us
    all_to_all x5, waiting for transfers between devices, scatter_sum(): lax.all_to_all(blocks, 'dp', 0, 0).astype(jnp.float32)  76.9 us
    all_to_all x4, blocking collectives, gather_rows(): return lax.all_to_all(copies, 'dp', 0, 0).reshape(-1, piece.shape[-1])  72 us
    all_to_all x3, blocking collectives, scatter_sum(): lax.all_to_all(blocks, 'dp', 0, 0).astype(jnp.float32)  63.4 us
    all_gather x1, waiting for transfers between devices, on_device(): enc_weight_out = lax.all_gather(enc_output[0], 'dec', axis=1, tiled=True)  47 us
    all_to_all x4, waiting for transfers between devices, gather_rows(): return lax.all_to_all(copies, 'dp', 0, 0).reshape(-1, piece.shape[-1])  42.8 us
    all_gather x1, waiting for transfers between devices, on_device(): enc_state = lax.all_gather(enc_piece, 'dp', axis=0, tiled=True)  34.5 us
    all_to_all x5, starting transfers between devices, scatter_sum(): lax.all_to_all(blocks, 'dp', 0, 0).astype(jnp.float32)  25.3 us
  transfers between devices with their start and end apart: 25, of which 16 were waited for; matrix products, arithmetic and copies ran while one was open for 5% of the time, Pallas kernels for 0%

profile of v1, /device:TPU:32, one launch (start us, length us, event | category | flops | bytes accessed | tf_op | source)
XLA Modules:
  0.0 616.0 jit_solution(11752825741048162005)
XLA Ops:
  8.1 0.7 all-gather.16.cloned.1.call-update
  8.8 0.7 all-gather.18.cloned.1.call-update
  11.2 120.7 %all-gather.16.cloned.1.call-done = bf16[1,4096,3,256]{3,1,2,0:T(8,128)(2,1)} async-done(((bf16[1,1024,3,256]{3,1,2,0:T(8,128)(2,1)}), bf16[1,4096,3,256]{3,1,2,0:T(8,128)(2,1)}) %all-gather.16.cloned.1.call-update) | async-done | bytes 6291472 | tf_op jit(solution)/shard_map/all_gather | solution.py:76
  131.9 3.8 fusion.63
  135.9 47.0 %all-gather.18.cloned.1.call-done = bf16[1,256,4096]{2,1,0:T(8,128)(2,1)} async-done(((bf16[1,256,1024]{2,1,0:T(8,128)(2,1)}), bf16[1,256,4096]{2,1,0:T(8,128)(2,1)}) %all-gather.18.cloned.1.call-update) | async-done | bytes 2097168 | tf_op jit(solution)/shard_map/all_gather | solution.py:77
  182.9 3.2 fusion.8
  186.1 6.8 %all-to-all-start = ((bf16[16,8,4096]{2,1,0:T(8,128)(2,1)}), bf16[16,8,4096]{2,1,0:T(8,128)(2,1)S(1)}, u32[]{:S(2)}, u32[]{:S(2)}) async-start(bf16[16,8,4096]{2,1,0:T(8,128)(2,1)} %fusion.8), calls=%async_computation | async-start | bytes 2097152 | tf_op jit(solution)/shard_map/all_to_all | solution.py:49
  192.9 15.9 %all-to-all-done = bf16[16,8,4096]{2,1,0:T(8,128)(2,1)S(1)} async-done(((bf16[16,8,4096]{2,1,0:T(8,128)(2,1)}), bf16[16,8,4096]{2,1,0:T(8,128)(2,1)S(1)}, u32[]{:S(2)}, u32[]{:S(2)}) %all-to-all-start) | async-done | bytes 1048608 | tf_op jit(solution)/shard_map/all_to_all | solution.py:49
  208.9 1.3 collective-permute-start
  210.2 0.9 collective-permute-done
  211.2 21.0 %all_to_all.80 = bf16[16,8,4096]{2,1,0:T(8,128)(2,1)S(1)} all-to-all(bf16[16,8,4096]{2,1,0:T(8,128)(2,1)S(1)} %broadcast_in_dim.69), channel_id=1, replica_groups=mesh['enc'=4,'dec'=4,'dp'=16] {'dp'}, dimensions={0} | all-to-all | bytes 2097152 | tf_op jit(solution)/shard_map/all_to_all | solution.py:43
  232.6 4.0 fusion.66
  237.5 2.4 fusion.9
  240.0 3.7 all-to-all-start.2
  243.7 2.3 copy.14
  246.0 14.1 %all-to-all-done.2 = bf16[16,8,4096]{2,1,0:T(8,128)(2,1)S(1)} async-done(((bf16[16,8,4096]{2,1,0:T(8,128)(2,1)}), bf16[16,8,4096]{2,1,0:T(8,128)(2,1)S(1)}, u32[]{:S(2)}, u32[]{:S(2)}) %all-to-all-start.2) | async-done | bytes 1048608 | tf_op jit(solution)/shard_map/all_to_all | solution.py:49
  261.1 16.3 %all_to_all.81 = bf16[16,8,4096]{2,1,0:T(8,128)(2,1)S(1)} all-to-all(bf16[16,8,4096]{2,1,0:T(8,128)(2,1)S(1)} %broadcast_in_dim.70), channel_id=1, replica_groups=mesh['enc'=4,'dec'=4,'dp'=16] {'dp'}, dimensions={0} | all-to-all | bytes 2097152 | tf_op jit(solution)/shard_map/all_to_all | solution.py:43
  277.8 3.8 fusion.69
  282.3 1.4 fusion.10
  283.8 17.6 %all_to_all.82 = bf16[16,8,4096]{2,1,0:T(8,128)(2,1)S(1)} all-to-all(bf16[16,8,4096]{2,1,0:T(8,128)(2,1)S(1)} %fusion.10), channel_id=1, replica_groups=mesh['enc'=4,'dec'=4,'dp'=16] {'dp'}, dimensions={0} | all-to-all | bytes 2097152 | tf_op jit(solution)/shard_map/all_to_all | solution.py:49
  302.2 1.1 broadcast_in_dim.71
  303.3 3.7 all-to-all-start.5
  307.6 14.8 %all-to-all-done.5 = bf16[16,8,4096]{2,1,0:T(8,128)(2,1)S(1)} async-done(((bf16[16,8,4096]{2,1,0:T(8,128)(2,1)}), bf16[16,8,4096]{2,1,0:T(8,128)(2,1)S(1)}, u32[]{:S(2)}, u32[]{:S(2)}) %all-to-all-start.5) | async-done | bytes 1048608 | tf_op jit(solution)/shard_map/all_to_all | solution.py:43
  322.8 3.8 fusion.72
  327.5 2.4 fusion.11
  329.9 6.1 all-to-all-start.6
  336.6 18.7 %all-to-all-done.6 = bf16[16,8,4096]{2,1,0:T(8,128)(2,1)S(1)} async-done(((bf16[16,8,4096]{2,1,0:T(8,128)(2,1)}), bf16[16,8,4096]{2,1,0:T(8,128)(2,1)S(1)}, u32[]{:S(2)}, u32[]{:S(2)}) %all-to-all-start.6) | async-done | bytes 1048608 | tf_op jit(solution)/shard_map/all_to_all | solution.py:49
  355.4 1.1 fusion.150
  357.3 1.3 collective-permute-start.4
  360.0 13.5 %collective-permute-done.4 = bf16[8,4096]{1,0:T(8,128)(2,1)S(1)} collective-permute-done((bf16[8,4096]{1,0:T(8,128)(2,1)S(1)}, bf16[8,4096]{1,0:T(8,128)(2,1)S(1)}, u32[]{:S(2)}, u32[]{:S(2)}) %collective-permute-start.4) | collective-permute-done | bytes 65568 | tf_op jit(solution)/shard_map/ppermute | solution.py:112
  373.6 1.1 broadcast_in_dim.72
  374.7 3.8 all-to-all-start.7
  379.5 12.4 %all-to-all-done.7 = bf16[16,8,4096]{2,1,0:T(8,128)(2,1)S(1)} async-done(((bf16[16,8,4096]{2,1,0:T(8,128)(2,1)}), bf16[16,8,4096]{2,1,0:T(8,128)(2,1)S(1)}, u32[]{:S(2)}, u32[]{:S(2)}) %all-to-all-start.7) | async-done | bytes 1048608 | tf_op jit(solution)/shard_map/all_to_all | solution.py:43
  391.9 2.9 fusion.75
  394.9 2.3 fusion.206
  397.2 5.6 all-gather.22.cloned.1.call-done
  402.8 2.2 fusion.12
  405.0 28.6 %all_to_all.83 = bf16[16,8,4096]{2,1,0:T(8,128)(2,1)S(1)} all-to-all(bf16[16,8,4096]{2,1,0:T(8,128)(2,1)S(1)} %fusion.12), channel_id=1, replica_groups=mesh['enc'=4,'dec'=4,'dp'=16] {'dp'}, dimensions={0} | all-to-all | bytes 2097152 | tf_op jit(solution)/shard_map/all_to_all | solution.py:49
  433.7 1.3 collective-permute-start.7
  435.0 4.9 collective-permute-done.7
  440.0 18.5 %all_to_all.84 = bf16[16,8,4096]{2,1,0:T(8,128)(2,1)S(1)} all-to-all(bf16[16,8,4096]{2,1,0:T(8,128)(2,1)S(1)} %broadcast_in_dim.73), channel_id=1, replica_groups=mesh['enc'=4,'dec'=4,'dp'=16] {'dp'}, dimensions={0} | all-to-all | bytes 2097152 | tf_op jit(solution)/shard_map/all_to_all | solution.py:43
  458.9 2.4 fusion.211
  461.9 17.3 %all_to_all.85 = bf16[16,8,4096]{2,1,0:T(8,128)(2,1)S(1)} all-to-all(bf16[16,8,4096]{2,1,0:T(8,128)(2,1)S(1)} %fusion.13), channel_id=1, replica_groups=mesh['enc'=4,'dec'=4,'dp'=16] {'dp'}, dimensions={0} | all-to-all | bytes 2097152 | tf_op jit(solution)/shard_map/all_to_all | solution.py:49
  479.4 1.3 collective-permute-start.8
  480.7 1.9 collective-permute-done.8
  482.7 16.2 %all_to_all.86 = bf16[16,8,4096]{2,1,0:T(8,128)(2,1)S(1)} all-to-all(bf16[16,8,4096]{2,1,0:T(8,128)(2,1)S(1)} %broadcast_in_dim.74), channel_id=1, replica_groups=mesh['enc'=4,'dec'=4,'dp'=16] {'dp'}, dimensions={0} | all-to-all | bytes 2097152 | tf_op jit(solution)/shard_map/all_to_all | solution.py:43
  499.3 2.3 fusion.216
  501.6 1.6 fusion.14
  503.2 3.8 all-to-all-start.12
  507.0 0.7 all-gather.12.cloned.1.call-update
  507.7 12.1 %all-to-all-done.12 = bf16[16,8,4096]{2,1,0:T(8,128)(2,1)S(1)} async-done(((bf16[16,8,4096]{2,1,0:T(8,128)(2,1)}), bf16[16,8,4096]{2,1,0:T(8,128)(2,1)S(1)}, u32[]{:S(2)}, u32[]{:S(2)}) %all-to-all-start.12) | async-done | bytes 1048608 | tf_op jit(solution)/shard_map/all_to_all | solution.py:49
  520.7 1.1 broadcast_in_dim.75
  521.8 3.7 all-to-all-start.13
  525.5 34.5 %all-gather.12.cloned.1.call-done = bf16[128,4096]{1,0:T(8,128)(2,1)} async-done(((bf16[8,4096]{1,0:T(8,128)(2,1)}), bf16[128,4096]{1,0:T(8,128)(2,1)}) %all-gather.12.cloned.1.call-update) | async-done | bytes 1048592 | tf_op jit(solution)/shard_map/all_gather | solution.py:122
  560.3 2.3 fusion.221
  562.6 1.6 fusion.15
  564.2 4.9 all-to-all-start.14
  569.2 16.1 %all-to-all-done.14 = bf16[16,8,4096]{2,1,0:T(8,128)(2,1)S(1)} async-done(((bf16[16,8,4096]{2,1,0:T(8,128)(2,1)}), bf16[16,8,4096]{2,1,0:T(8,128)(2,1)S(1)}, u32[]{:S(2)}, u32[]{:S(2)}) %all-to-all-start.14) | async-done | bytes 1048608 | tf_op jit(solution)/shard_map/all_to_all | solution.py:49
  585.4 1.0 fusion.154
  586.4 1.1 broadcast_in_dim.144
  587.5 3.7 all-to-all-start.15
  591.1 15.6 %all-to-all-done.15 = bf16[16,8,4096]{2,1,0:T(8,128)(2,1)S(1)} async-done(((bf16[16,8,4096]{2,1,0:T(8,128)(2,1)}), bf16[16,8,4096]{2,1,0:T(8,128)(2,1)S(1)}, u32[]{:S(2)}, u32[]{:S(2)}) %all-to-all-start.15) | async-done | bytes 1048608 | tf_op jit(solution)/shard_map/all_to_all | solution.py:43
  606.8 1.0 copy.17
  607.7 1.0 copy.18
  (122 shorter events, 15.5 us)
Async XLA Ops:
  8.0 1.5 copy-start.14
  8.0 2.8 copy-start.3
  8.0 123.9 %copy-start.15 = (f32[1,4096]{1,0:T(1,128)S(1)}, f32[1,4096]{1,0:T(1,128)}, u32[]{:S(2)}) copy-start(f32[1,4096]{1,0:T(1,128)} %param.14) | copy-start | bytes 49156
  8.0 123.8 %all-gather.16.cloned.1.call-start = ((), (), s32[]{:S(2)}) async-start(), calls=%async_computation.18 | async-start | bytes 7864320 | tf_op jit(solution)/shard_map/all_gather | solution.py:76
  8.8 174.1 %all-gather.18.cloned.1.call-start = ((), (), s32[]{:S(2)}) async-start(), calls=%async_computation.19 | async-start | bytes 2621440 | tf_op jit(solution)/shard_map/all_gather | solution.py:77
  186.1 22.7 %all-to-all-start = ((bf16[16,8,4096]{2,1,0:T(8,128)(2,1)}), bf16[16,8,4096]{2,1,0:T(8,128)(2,1)S(1)}, u32[]{:S(2)}, u32[]{:S(2)}) async-start(bf16[16,8,4096]{2,1,0:T(8,128)(2,1)} %fusion.8), calls=%async_computation | async-start | bytes 2097152 | tf_op jit(solution)/shard_map/all_to_all | solution.py:49
  208.9 2.2 collective-permute-start
  232.6 4.9 copy-start.1
  236.6 0.7 copy-start.12
  240.0 20.2 %all-to-all-start.2 = ((bf16[16,8,4096]{2,1,0:T(8,128)(2,1)}), bf16[16,8,4096]{2,1,0:T(8,128)(2,1)S(1)}, u32[]{:S(2)}, u32[]{:S(2)}) async-start(bf16[16,8,4096]{2,1,0:T(8,128)(2,1)} %fusion.9), calls=%async_computation.2 | async-start | bytes 2097152 | tf_op jit(solution)/shard_map/all_to_all | solution.py:49
  243.6 135.9 %all-gather.20.cloned.1.call-start = ((), (), s32[]{:S(2)}) async-start(), calls=%async_computation.20 | async-start | bytes 5242880 | tf_op jit(solution)/shard_map/all_gather | solution.py:78
  260.3 0.7 collective-permute-start.1
  281.6 0.7 copy-start.13
  301.5 0.7 collective-permute-start.2
  303.3 19.1 %all-to-all-start.5 = ((bf16[16,8,4096]{2,1,0:T(8,128)(2,1)}), bf16[16,8,4096]{2,1,0:T(8,128)(2,1)S(1)}, u32[]{:S(2)}, u32[]{:S(2)}) async-start(bf16[16,8,4096]{2,1,0:T(8,128)(2,1)} %broadcast_in_dim.71), calls=%async_computation.5 | async-start | bytes 2097152 | tf_op jit(solution)/shard_map/all_to_all | solution.py:43
  307.0 87.9 %all-gather.14.cloned.1.call-start = ((), (), s32[]{:S(2)}) async-start(), calls=%async_computation.17 | async-start | bytes 2621440 | tf_op jit(solution)/shard_map/all_gather | solution.py:79
  326.6 0.7 copy-start.11
  329.9 26.6 %copy-start.10 = (f32[4096]{0:T(1024)S(1)}, f32[4096]{0:T(1024)}, u32[]{:S(2)}) copy-start(f32[4096]{0:T(1024)} %param.17) | copy-start | bytes 49156
  329.9 25.3 %all-to-all-start.6 = ((bf16[16,8,4096]{2,1,0:T(8,128)(2,1)}), bf16[16,8,4096]{2,1,0:T(8,128)(2,1)S(1)}, u32[]{:S(2)}, u32[]{:S(2)}) async-start(bf16[16,8,4096]{2,1,0:T(8,128)(2,1)} %fusion.11), calls=%async_computation.6 | async-start | bytes 2097152 | tf_op jit(solution)/shard_map/all_to_all | solution.py:49
  336.0 66.8 %all-gather.22.cloned.1.call-start = ((), (), s32[]{:S(2)}) async-start(), calls=%async_computation.21 | async-start | bytes 2621440 | tf_op jit(solution)/shard_map/all_gather | solution.py:80
  355.4 23.7 %copy-start.2 = (bf16[1,128,4096]{2,1,0:T(8,128)(2,1)S(1)}, bf16[1,128,4096]{2,1,0:T(8,128)(2,1)}, u32[]{:S(2)}) copy-start(bf16[1,128,4096]{2,1,0:T(8,128)(2,1)} %param.12) | copy-start | bytes 3145732
  356.5 22.9 %copy-start.5 = (bf16[8,4096]{1,0:T(8,128)(2,1)}, bf16[8,4096]{1,0:T(8,128)(2,1)S(1)}, u32[]{:S(2)}) copy-start(bf16[8,4096]{1,0:T(8,128)(2,1)S(1)} %get-tuple-element.9) | copy-start | bytes 196612
  356.7 3.3 collective-permute-start.3
  357.3 16.2 %collective-permute-start.4 = (bf16[8,4096]{1,0:T(8,128)(2,1)S(1)}, bf16[8,4096]{1,0:T(8,128)(2,1)S(1)}, u32[]{:S(2)}, u32[]{:S(2)}) collective-permute-start(bf16[8,4096]{1,0:T(8,128)(2,1)S(1)} %fusion.152), channel_id=1, source_target_pairs={{192,16},{193,17},{194,18},{195,19},{196,20},{197,21},{198,22},{19... | collective-permute-start | bytes 196616 | tf_op jit(solution)/shard_map/ppermute | solution.py:112
  358.6 14.9 %collective-permute-start.5 = (bf16[8,4096]{1,0:T(8,128)(2,1)S(1)}, bf16[8,4096]{1,0:T(8,128)(2,1)S(1)}, u32[]{:S(2)}, u32[]{:S(2)}) collective-permute-start(bf16[8,4096]{1,0:T(8,128)(2,1)S(1)} %fusion.152), channel_id=1, source_target_pairs={{192,32},{193,33},{194,34},{195,35},{196,36},{197,37},{198,38},{19... | collective-permute-start | bytes 196616 | tf_op jit(solution)/shard_map/ppermute | solution.py:112
  359.3 14.2 %collective-permute-start.6 = (bf16[8,4096]{1,0:T(8,128)(2,1)S(1)}, bf16[8,4096]{1,0:T(8,128)(2,1)S(1)}, u32[]{:S(2)}, u32[]{:S(2)}) collective-permute-start(bf16[8,4096]{1,0:T(8,128)(2,1)S(1)} %fusion.152), channel_id=1, source_target_pairs={{192,48},{193,49},{194,50},{195,51},{196,52},{197,53},{198,54},{19... | collective-permute-start | bytes 196616 | tf_op jit(solution)/shard_map/ppermute | solution.py:112
  374.7 17.2 %all-to-all-start.7 = ((bf16[16,8,4096]{2,1,0:T(8,128)(2,1)}), bf16[16,8,4096]{2,1,0:T(8,128)(2,1)S(1)}, u32[]{:S(2)}, u32[]{:S(2)}) async-start(bf16[16,8,4096]{2,1,0:T(8,128)(2,1)} %broadcast_in_dim.72), calls=%async_computation.7 | async-start | bytes 2097152 | tf_op jit(solution)/shard_map/all_to_all | solution.py:43
  379.2 79.7 %copy-start.17 = (pred[128]{0:T(512)(128)(4,1)}, pred[128]{0:T(512)(128)(4,1)S(1)}, u32[]{:S(2)}) copy-start(pred[128]{0:T(512)(128)(4,1)S(1)} %iota_compare_fusion.1) | copy-start | bytes 388
  379.5 15.4 %copy-start.16 = (f32[1,4096]{1,0:T(1,128)S(1)}, f32[1,4096]{1,0:T(1,128)}, u32[]{:S(2)}) copy-start(f32[1,4096]{1,0:T(1,128)} %param.18) | copy-start | bytes 49156
  433.7 6.2 collective-permute-start.7
  458.7 2.6 copy-start
  479.4 19.9 %copy-start.18 = (pred[128]{0:T(512)(128)(4,1)S(1)}, pred[128]{0:T(512)(128)(4,1)}, u32[]{:S(2)}) copy-start(pred[128]{0:T(512)(128)(4,1)} %copy-done.17) | copy-start | bytes 388
  479.4 3.2 collective-permute-start.8
  482.6 16.6 %copy-start.8 = (bf16[8,4096]{1,0:T(8,128)(2,1)}, bf16[8,4096]{1,0:T(8,128)(2,1)S(1)}, u32[]{:S(2)}) copy-start(bf16[8,4096]{1,0:T(8,128)(2,1)S(1)} %collective-permute-done.8) | copy-start | bytes 196612
  503.2 16.8 %copy-start.9 = (bf16[8,4096]{1,0:T(8,128)(2,1)S(1)}, bf16[8,4096]{1,0:T(8,128)(2,1)}, u32[]{:S(2)}) copy-start(bf16[8,4096]{1,0:T(8,128)(2,1)} %copy-done.8) | copy-start | bytes 196612
  503.2 16.7 %all-to-all-start.12 = ((bf16[16,8,4096]{2,1,0:T(8,128)(2,1)}), bf16[16,8,4096]{2,1,0:T(8,128)(2,1)S(1)}, u32[]{:S(2)}, u32[]{:S(2)}) async-start(bf16[16,8,4096]{2,1,0:T(8,128)(2,1)} %fusion.14), calls=%async_computation.12 | async-start | bytes 2097152 | tf_op jit(solution)/shard_map/all_to_all | solution.py:49
  507.0 53.0 %all-gather.12.cloned.1.call-start = ((), (), s32[]{:S(2)}) async-start(), calls=%async_computation.16 | async-start | bytes 1114112 | tf_op jit(solution)/shard_map/all_gather | solution.py:122
  520.0 40.2 %copy-start.6 = (bf16[8,4096]{1,0:T(8,128)(2,1)}, bf16[8,4096]{1,0:T(8,128)(2,1)S(1)}, u32[]{:S(2)}) copy-start(bf16[8,4096]{1,0:T(8,128)(2,1)S(1)} %add_convert_fusion.1) | copy-start | bytes 196612
  520.0 40.2 %copy-start.19 = (pred[128]{0:T(512)(128)(4,1)S(1)}, pred[128]{0:T(512)(128)(4,1)}, u32[]{:S(2)}) copy-start(pred[128]{0:T(512)(128)(4,1)} %copy-done.17) | copy-start | bytes 388
  520.0 0.7 collective-permute-start.9
  521.8 38.2 %all-to-all-start.13 = ((bf16[16,8,4096]{2,1,0:T(8,128)(2,1)}), bf16[16,8,4096]{2,1,0:T(8,128)(2,1)S(1)}, u32[]{:S(2)}, u32[]{:S(2)}) async-start(bf16[16,8,4096]{2,1,0:T(8,128)(2,1)} %broadcast_in_dim.75), calls=%async_computation.13 | async-start | bytes 2097152 | tf_op jit(solution)/shard_map/all_to_all | solution.py:43
  564.2 21.2 %copy-start.7 = (bf16[8,4096]{1,0:T(8,128)(2,1)S(1)}, bf16[8,4096]{1,0:T(8,128)(2,1)}, u32[]{:S(2)}) copy-start(bf16[8,4096]{1,0:T(8,128)(2,1)} %copy-done.6) | copy-start | bytes 196612
  564.2 21.1 %all-to-all-start.14 = ((bf16[16,8,4096]{2,1,0:T(8,128)(2,1)}), bf16[16,8,4096]{2,1,0:T(8,128)(2,1)S(1)}, u32[]{:S(2)}, u32[]{:S(2)}) async-start(bf16[16,8,4096]{2,1,0:T(8,128)(2,1)} %fusion.15), calls=%async_computation.14 | async-start | bytes 2097152 | tf_op jit(solution)/shard_map/all_to_all | solution.py:49
  585.4 21.3 %copy-start.4 = (bf16[128,4096]{1,0:T(8,128)(2,1)S(1)}, bf16[128,4096]{1,0:T(8,128)(2,1)}, u32[]{:S(2)}) copy-start(bf16[128,4096]{1,0:T(8,128)(2,1)} %all-gather.12.cloned.1.call-done) | copy-start | bytes 3145732
  587.5 19.3 %all-to-all-start.15 = ((bf16[16,8,4096]{2,1,0:T(8,128)(2,1)}), bf16[16,8,4096]{2,1,0:T(8,128)(2,1)S(1)}, u32[]{:S(2)}, u32[]{:S(2)}) async-start(bf16[16,8,4096]{2,1,0:T(8,128)(2,1)} %broadcast_in_dim.144), calls=%async_computation.15 | async-start | bytes 2097152 | tf_op jit(solution)/shard_map/all_to_all | solution.py:43
Sparse Core Ops, SparseCore 0:
  10.7 121.1 all-gather.15
  133.7 49.1 all-gather.17
  510.2 49.6 all-gather.11
Sparse Core Ops, SparseCore 1:
  246.5 65.3 all-gather.19
  313.5 52.5 all-gather.13
  367.8 34.9 all-gather.21
